TPU v7x, 32 devices: a whole 2x2x4 slice. The times are simulated.
32 devices in a mesh: dp: 16 (over z, y, x), tensor: 2 (over core).
Axes of the slice: x: 2, y: 2, z: 4, core: 2. Of those that a mesh axis runs over, the one named last changes fastest.
Arguments:
- hidden_in: bfloat16 [32768, 768], P(('dp', 'tensor')), may hold values from -6 to 6
- out_grad: bfloat16 [32768, 768], P(('dp', 'tensor')), may hold values from -6 to 6
- seq_lengths: int32 [16, 8], P('dp'), may hold values from 1 to 1024, as said below
- attn_gain: bfloat16 [768], P('dp'), may hold values from 0.099609375 to 1.8984375
- attn_shift: bfloat16 [768], P('dp'), may hold values from -1.75 to 1.75
- mlp_gain: bfloat16 [768], P('dp'), may hold values from 0.099609375 to 1.8984375
- mlp_shift: bfloat16 [768], P('dp'), may hold values from -1.75 to 1.75
- qkv_weight: bfloat16 [768, 12, 192], P('dp', 'tensor'), may hold values from -0.21875 to 0.21875
- qkv_bias: bfloat16 [2304], P('dp'), may hold values from -1.75 to 1.75
- dense_weight: bfloat16 [768, 12, 64], P('dp', 'tensor'), may hold values from -0.875 to 0.875
- dense_bias: bfloat16 [768], P('dp'), may hold values from -1.75 to 1.75
- fc_weight: bfloat16 [768, 3072], P('dp', 'tensor'), may hold values from -0.21875 to 0.21875
- fc_bias: bfloat16 [3072], P('dp'), may hold values from -1.75 to 1.75
- proj_weight: bfloat16 [768, 3072], P('dp', 'tensor'), may hold values from -0.15625 to 0.15625
- proj_bias: bfloat16 [768], P('dp'), may hold values from -1.75 to 1.75
Outputs:
- block_out: bfloat16 [32768, 768], P(('dp', 'tensor'))
- input_grad: float32 [32768, 768], P(('dp', 'tensor'))
- attn_gain_grad: float32 [768], P(('dp', 'tensor'))
- attn_shift_grad: float32 [768], P(('dp', 'tensor'))
- mlp_gain_grad: float32 [768], P(('dp', 'tensor'))
- mlp_shift_grad: float32 [768], P(('dp', 'tensor'))
- qkv_weight_grad: float32 [768, 12, 192], P('dp', 'tensor')
- qkv_bias_grad: float32 [2304], P(('dp', 'tensor'))
- dense_weight_grad: float32 [768, 12, 64], P('dp', 'tensor')
- dense_bias_grad: float32 [768], P(('dp', 'tensor'))
- fc_weight_grad: float32 [768, 3072], P('dp', 'tensor')
- fc_bias_grad: float32 [3072], P(('dp', 'tensor'))
- proj_weight_grad: float32 [768, 3072], P('dp', 'tensor')
- proj_bias_grad: float32 [768], P(('dp', 'tensor'))
Inputs may be any that keep to these rules, and one draw needn't show every extreme that they name: `seq_lengths`: row g lists the 8 sequences of group g in order; they are all 1 or longer and sum to 2048. One sequence of each row has exactly 1024 rows and covers rows 1023 and 1024 of its group.
All inputs are finite; a program needn't handle non-finite values.
Results may differ from a plain program's by a relative error of at most 0.012.
Values may be sent and summed in bfloat16 or wider, within the bound.
A program may use at most 256 MiB of HBM per device.

v0:
```python
import jax
import jax.numpy as jnp
from jax import lax
from jax.sharding import PartitionSpec as P


def layout(lengths, group_rows):
    seq_index = jnp.arange(lengths.shape[0], dtype=jnp.int32)
    seq_ends = jnp.sum(
        jnp.where(seq_index[None, :] <= seq_index[:, None], lengths[None, :], 0), axis=1
    )
    starts = seq_ends - lengths
    row_index = jnp.arange(group_rows, dtype=jnp.int32)
    seg_ids = jnp.sum((row_index[:, None] >= seq_ends[None, :]).astype(jnp.int32), axis=1)
    owner_mask = seg_ids[:, None] == jnp.arange(lengths.shape[0], dtype=jnp.int32)[None, :]
    positions = row_index - jnp.sum(jnp.where(owner_mask, starts[None, :], 0), axis=1)
    return (seg_ids, positions)


def layer_norm(values, gain_vec, shift_vec):
    average = jnp.mean(values, axis=-1, keepdims=True)
    centred = values - average
    spread = jnp.mean(centred * centred, axis=-1, keepdims=True)
    return centred * lax.rsqrt(spread + 1e-05) * gain_vec + shift_vec


def rotary_tables(positions, head_dim):
    rot_dims = head_dim // 4
    half_rot = rot_dims // 2
    inv_freq = 10000.0 ** (-(jnp.arange(half_rot, dtype=jnp.float32) * 2.0 / rot_dims))
    angles = positions.astype(jnp.float32)[:, None] * inv_freq[None, :]
    angles = jnp.concatenate([angles, angles], axis=-1)
    return (jnp.cos(angles), jnp.sin(angles))


def rotate(vectors, cosine_table, sine_table):
    rot_dims = cosine_table.shape[-1]
    half_rot = rot_dims // 2
    rot_part = vectors[..., :rot_dims]
    turned = jnp.concatenate([-rot_part[..., half_rot:], rot_part[..., :half_rot]], axis=-1)
    result = rot_part * cosine_table[:, None, :] + turned * sine_table[:, None, :]
    return jnp.concatenate([result, vectors[..., rot_dims:]], axis=-1)


def exact_gelu(values):
    return jax.nn.gelu(values, approximate=False)


def body(
    hidden_in,
    out_grad,
    seq_lengths,
    attn_gain,
    attn_shift,
    mlp_gain,
    mlp_shift,
    qkv_weight,
    qkv_bias,
    dense_weight,
    dense_bias,
    fc_weight,
    fc_bias,
    proj_weight,
    proj_bias,
):
    tensor_index = lax.axis_index("tensor")
    tensor_count = lax.axis_size("tensor")
    local_rows = hidden_in.shape[0]
    group_rows = local_rows * tensor_count
    gathered = (
        lax.all_gather(qkv_weight, "dp", axis=0, tiled=True),
        lax.all_gather(dense_weight, "dp", axis=0, tiled=True),
        lax.all_gather(fc_weight, "dp", axis=0, tiled=True),
        lax.all_gather(proj_weight, "dp", axis=0, tiled=True),
        lax.all_gather(attn_gain, "dp", axis=0, tiled=True),
        lax.all_gather(attn_shift, "dp", axis=0, tiled=True),
        lax.all_gather(mlp_gain, "dp", axis=0, tiled=True),
        lax.all_gather(mlp_shift, "dp", axis=0, tiled=True),
        lax.all_gather(qkv_bias, "dp", axis=0, tiled=True),
        lax.all_gather(dense_bias, "dp", axis=0, tiled=True),
        lax.all_gather(fc_bias, "dp", axis=0, tiled=True),
        lax.all_gather(proj_bias, "dp", axis=0, tiled=True),
    )
    (
        w_qkv,
        w_dense,
        w_fc,
        w_proj,
        gain_attn,
        shift_attn,
        gain_mlp,
        shift_mlp,
        bias_qkv,
        bias_dense,
        bias_fc,
        bias_proj,
    ) = gathered
    model_width = w_qkv.shape[0]
    head_count = w_qkv.shape[1]
    triple_width = w_qkv.shape[2]
    head_dim = w_dense.shape[2]
    hidden_units = w_fc.shape[1]
    qkv_cols = head_count * triple_width
    attn_cols = head_count * head_dim
    my_bias_qkv = lax.dynamic_slice_in_dim(bias_qkv, tensor_index * qkv_cols, qkv_cols).astype(
        jnp.float32
    )
    my_bias_fc = lax.dynamic_slice_in_dim(
        bias_fc, tensor_index * hidden_units, hidden_units
    ).astype(jnp.float32)
    gain_attn_f = gain_attn.astype(jnp.float32)
    shift_attn_f = shift_attn.astype(jnp.float32)
    gain_mlp_f = gain_mlp.astype(jnp.float32)
    shift_mlp_f = shift_mlp.astype(jnp.float32)
    seg_ids, positions = layout(seq_lengths[0], group_rows)
    x_rows = hidden_in.astype(jnp.float32)

    def norms(values, gain_one, shift_one, gain_two, shift_two):
        return (layer_norm(values, gain_one, shift_one), layer_norm(values, gain_two, shift_two))

    (normed_one, normed_two), norm_back = jax.vjp(
        norms, x_rows, gain_attn_f, shift_attn_f, gain_mlp_f, shift_mlp_f
    )
    normed_attn, normed_mlp = (
        lax.all_gather(normed_one.astype(jnp.bfloat16), "tensor", axis=0, tiled=True),
        lax.all_gather(normed_two.astype(jnp.bfloat16), "tensor", axis=0, tiled=True),
    )
    merged_lin = (
        jnp.dot(
            normed_attn, w_qkv.reshape(model_width, qkv_cols), preferred_element_type=jnp.float32
        )
        + my_bias_qkv
    )
    merged_lin = merged_lin.reshape(group_rows, head_count, triple_width)
    cosine_table, sine_table = rotary_tables(positions, head_dim)

    def turn_pair(query_lin, key_lin):
        return (
            rotate(query_lin, cosine_table, sine_table),
            rotate(key_lin, cosine_table, sine_table),
        )

    (query_rot, key_rot), turn_back = jax.vjp(
        turn_pair, merged_lin[..., :head_dim], merged_lin[..., head_dim : 2 * head_dim]
    )
    query_low = query_rot.astype(jnp.bfloat16)
    key_low = key_rot.astype(jnp.bfloat16)
    value_low = merged_lin[..., 2 * head_dim :].astype(jnp.bfloat16)
    score_scale = head_dim ** (-0.5)
    block_rows = min(512, group_rows)
    block_count = group_rows // block_rows
    row_index = jnp.arange(group_rows, dtype=jnp.int32)

    def masked_scores(number):
        begin_row = number * block_rows
        end_row = begin_row + block_rows
        scores = (
            jnp.einsum(
                "qhd,khd->hqk",
                query_low[begin_row:end_row],
                key_low[:end_row],
                preferred_element_type=jnp.float32,
            )
            * score_scale
        )
        allowed = (row_index[None, :end_row] <= row_index[begin_row:end_row, None]) & (
            seg_ids[None, :end_row] == seg_ids[begin_row:end_row, None]
        )
        return jnp.where(allowed[None], scores, -1e30)

    head_blocks = []
    log_totals = []
    for number in range(block_count):
        end_row = (number + 1) * block_rows
        scores = masked_scores(number)
        peak_score = jnp.max(scores, axis=-1, keepdims=True)
        weights = jnp.exp(scores - peak_score)
        norm_total = jnp.sum(weights, axis=-1, keepdims=True)
        log_totals.append(peak_score + jnp.log(norm_total))
        prob_low = (weights / norm_total).astype(jnp.bfloat16)
        head_blocks.append(
            jnp.einsum(
                "hqk,khd->qhd", prob_low, value_low[:end_row], preferred_element_type=jnp.float32
            )
        )
    heads_flat = (
        jnp.concatenate(head_blocks, axis=0).astype(jnp.bfloat16).reshape(group_rows, attn_cols)
    )
    attn_part = jnp.einsum(
        "gc,dc->gd",
        heads_flat,
        w_dense.reshape(model_width, attn_cols),
        preferred_element_type=jnp.float32,
    )
    fc_pre = jnp.dot(normed_mlp, w_fc, preferred_element_type=jnp.float32) + my_bias_fc
    act_full, gelu_back = jax.vjp(exact_gelu, fc_pre)
    act_low = act_full.astype(jnp.bfloat16)
    mlp_part = jnp.einsum("gf,df->gd", act_low, w_proj, preferred_element_type=jnp.float32)
    branch_rows = lax.psum_scatter(
        (attn_part + mlp_part).astype(jnp.bfloat16), "tensor", scatter_dimension=0, tiled=True
    ).astype(jnp.float32)
    block_out = (
        x_rows + branch_rows + bias_dense.astype(jnp.float32) + bias_proj.astype(jnp.float32)
    ).astype(jnp.bfloat16)
    w_qkv, w_dense, w_fc, w_proj = (
        lax.all_gather(qkv_weight, "dp", axis=0, tiled=True),
        lax.all_gather(dense_weight, "dp", axis=0, tiled=True),
        lax.all_gather(fc_weight, "dp", axis=0, tiled=True),
        lax.all_gather(proj_weight, "dp", axis=0, tiled=True),
    )
    cot_all = lax.all_gather(out_grad, "tensor", axis=0, tiled=True)
    grad_act = jnp.dot(cot_all, w_proj, preferred_element_type=jnp.float32)
    grad_proj = jnp.einsum("gd,gf->df", cot_all, act_low, preferred_element_type=jnp.float32)
    grad_pre = gelu_back(grad_act)[0].astype(jnp.bfloat16)
    grad_fc = jnp.einsum("gd,gf->df", normed_mlp, grad_pre, preferred_element_type=jnp.float32)
    fc_bias_part = jnp.sum(grad_pre, axis=0, dtype=jnp.float32)
    grad_normed_mlp = jnp.einsum("gf,df->gd", grad_pre, w_fc, preferred_element_type=jnp.float32)
    dense_flat = w_dense.reshape(model_width, attn_cols)
    grad_heads = (
        jnp.dot(cot_all, dense_flat, preferred_element_type=jnp.float32)
        .astype(jnp.bfloat16)
        .reshape(group_rows, head_count, head_dim)
    )
    grad_dense = jnp.einsum(
        "gd,gc->dc", cot_all, heads_flat, preferred_element_type=jnp.float32
    ).reshape(model_width, head_count, head_dim)
    query_grads = []
    grad_key = jnp.zeros((group_rows, head_count, head_dim), jnp.float32)
    grad_value = jnp.zeros((group_rows, head_count, head_dim), jnp.float32)
    for number in range(block_count):
        begin_row = number * block_rows
        end_row = begin_row + block_rows
        probs = jnp.exp(masked_scores(number) - log_totals[number])
        heads_blk = grad_heads[begin_row:end_row]
        grad_probs = jnp.einsum(
            "qhd,khd->hqk", heads_blk, value_low[:end_row], preferred_element_type=jnp.float32
        )
        row_delta = jnp.sum(probs * grad_probs, axis=-1, keepdims=True)
        grad_scores = (probs * (grad_probs - row_delta)).astype(jnp.bfloat16)
        query_grads.append(
            jnp.einsum(
                "hqk,khd->qhd", grad_scores, key_low[:end_row], preferred_element_type=jnp.float32
            )
            * score_scale
        )
        grad_key = grad_key.at[:end_row].add(
            jnp.einsum(
                "hqk,qhd->khd",
                grad_scores,
                query_low[begin_row:end_row],
                preferred_element_type=jnp.float32,
            )
            * score_scale
        )
        grad_value = grad_value.at[:end_row].add(
            jnp.einsum(
                "hqk,qhd->khd",
                probs.astype(jnp.bfloat16),
                heads_blk,
                preferred_element_type=jnp.float32,
            )
        )
    grad_query = jnp.concatenate(query_grads, axis=0)
    grad_query_lin, grad_key_lin = turn_back((grad_query, grad_key))
    grad_merged = (
        jnp.concatenate([grad_query_lin, grad_key_lin, grad_value], axis=-1)
        .astype(jnp.bfloat16)
        .reshape(group_rows, qkv_cols)
    )
    grad_qkv = jnp.einsum(
        "gd,gc->dc", normed_attn, grad_merged, preferred_element_type=jnp.float32
    ).reshape(model_width, head_count, triple_width)
    qkv_bias_part = jnp.sum(grad_merged, axis=0, dtype=jnp.float32)
    grad_normed_attn = jnp.einsum(
        "gc,dc->gd",
        grad_merged,
        w_qkv.reshape(model_width, qkv_cols),
        preferred_element_type=jnp.float32,
    )
    cot_rows = out_grad.astype(jnp.float32)
    local_attn, local_mlp = (
        lax.psum_scatter(
            grad_normed_attn.astype(jnp.bfloat16), "tensor", scatter_dimension=0, tiled=True
        ).astype(jnp.float32),
        lax.psum_scatter(
            grad_normed_mlp.astype(jnp.bfloat16), "tensor", scatter_dimension=0, tiled=True
        ).astype(jnp.float32),
    )
    grad_x, grad_gain_attn, grad_shift_attn, grad_gain_mlp, grad_shift_mlp = norm_back(
        (local_attn, local_mlp)
    )
    input_grad = cot_rows + grad_x
    cot_sums = jnp.sum(cot_rows, axis=0)
    full_qkv_bias = lax.dynamic_update_slice_in_dim(
        jnp.zeros((qkv_cols * tensor_count,), jnp.float32),
        qkv_bias_part,
        tensor_index * qkv_cols,
        0,
    )
    full_fc_bias = lax.dynamic_update_slice_in_dim(
        jnp.zeros((hidden_units * tensor_count,), jnp.float32),
        fc_bias_part,
        tensor_index * hidden_units,
        0,
    )
    small_sums = (
        lax.psum_scatter(grad_gain_attn, ("dp", "tensor"), scatter_dimension=0, tiled=True),
        lax.psum_scatter(grad_shift_attn, ("dp", "tensor"), scatter_dimension=0, tiled=True),
        lax.psum_scatter(grad_gain_mlp, ("dp", "tensor"), scatter_dimension=0, tiled=True),
        lax.psum_scatter(grad_shift_mlp, ("dp", "tensor"), scatter_dimension=0, tiled=True),
        lax.psum_scatter(full_qkv_bias, ("dp", "tensor"), scatter_dimension=0, tiled=True),
        lax.psum_scatter(cot_sums, ("dp", "tensor"), scatter_dimension=0, tiled=True),
        lax.psum_scatter(full_fc_bias, ("dp", "tensor"), scatter_dimension=0, tiled=True),
    )
    large_sums = (
        lax.psum_scatter(grad_qkv, "dp", scatter_dimension=0, tiled=True),
        lax.psum_scatter(grad_dense, "dp", scatter_dimension=0, tiled=True),
        lax.psum_scatter(grad_fc, "dp", scatter_dimension=0, tiled=True),
        lax.psum_scatter(grad_proj, "dp", scatter_dimension=0, tiled=True),
    )
    return (
        block_out,
        input_grad,
        small_sums[0],
        small_sums[1],
        small_sums[2],
        small_sums[3],
        large_sums[0],
        small_sums[4],
        large_sums[1],
        small_sums[5],
        large_sums[2],
        small_sums[6],
        large_sums[3],
        small_sums[5],
    )


def solution(mesh):
    in_specs = (
        P(("dp", "tensor"), None),
        P(("dp", "tensor"), None),
        P("dp", None),
        P("dp"),
        P("dp"),
        P("dp"),
        P("dp"),
        P("dp", "tensor", None),
        P("dp"),
        P("dp", "tensor", None),
        P("dp"),
        P("dp", "tensor"),
        P("dp"),
        P("dp", "tensor"),
        P("dp"),
    )
    out_specs = (
        P(("dp", "tensor"), None),
        P(("dp", "tensor"), None),
        P(("dp", "tensor")),
        P(("dp", "tensor")),
        P(("dp", "tensor")),
        P(("dp", "tensor")),
        P("dp", "tensor", None),
        P(("dp", "tensor")),
        P("dp", "tensor", None),
        P(("dp", "tensor")),
        P("dp", "tensor"),
        P(("dp", "tensor")),
        P("dp", "tensor"),
        P(("dp", "tensor")),
    )
    return jax.shard_map(body, mesh=mesh, in_specs=in_specs, out_specs=out_specs, check_vma=False)
```

profile of v0, /device:TPU:0, one launch (start us, length us, event | category | flops | bytes accessed | tf_op | source)
XLA Modules:
  0.0 1065.3 jit_solution(10863352786644890494)
XLA Ops:
  18.7 79.0 %all-reduce.26 = (bf16[768]{0:T(1024)(128)(2,1)S(1)}, bf16[768]{0:T(1024)(128)(2,1)S(1)}, bf16[3072]{0:T(1024)(128)(2,1)S(1)}, bf16[768]{0:T(1024)(128)(2,1)S(1)...) all-reduce(bf16[768]{0:T(1024)(128)(2,1)S(1)} %dynamic-update-slice, ...), channel_id=1, replica_groups=mesh['dp'=16,'tensor'=2] {'dp'}, use_global_device_ids=true, to_apply=%add.14 | all-reduce | flops 9984 | bytes 39936
  105.8 44.1 %all_gather.54 = bf16[768,6,64]{2,0,1:T(8,128)(2,1)S(1)} all-gather(bf16[48,6,64]{2,0,1:T(8,128)(2,1)S(1)} %copy-done.50), channel_id=1, replica_groups=mesh['dp'=16,'tensor'=2] {'dp'}, dimensions={0}, use_global_device_ids=true | all-gather | bytes 626688 | tf_op jit(solution)/shard_map/all_gather | solution.py:72
  200.7 6.3 multiply_convert_fusion.2
  211.7 8.4 fusion.153
  220.1 9.0 fusion.2
  229.1 12.9 %multiply_reduce_fusion.1 = (f32[6,512]{1,0:T(8,128)S(1)}, f32[6,512,1536]{2,1,0:T(8,128)}) fusion(f32[6,512,1536]{2,1,0:T(8,128)} %get-tuple-element.251, f32[6,512]{1,0:T(8,128)S(1)} %log_add_fusion.1, bf16[512,6,64]{0,2,1:T(8,128)(2,1)} %bitcast.137, bf16[2048,6,192]{0,2,1:T(8,128)(2,1)} %copy-done.9), kind=kOutput, calls=%fused_computation.10 | convolution fusion | flops 618132480 | bytes 39346176 | tf_op jit(solution)/shard_map/qhd,khd->hqk/dot_general | solution.py:235
  242.1 13.0 %multiply_convert_fusion.1 = bf16[6,512,1536]{2,1,0:T(8,128)(2,1)S(1)} fusion(f32[6,512,1536]{2,1,0:T(8,128)} %get-tuple-element.257, f32[6,512,1536]{2,1,0:T(8,128)} %get-tuple-element.251, f32[6,512]{1,0:T(8,128)S(1)} %get-tuple-element.256, f32[6,512]{1,0:T(8,128)S(1)} %log_add_fusion.1), kind=kLoop, calls=%fused_computation.9 | loop fusion | flops 18874368 | bytes 47210496 | tf_op jit(solution)/shard_map/convert_element_type | solution.py:239
  260.8 10.7 %fusion.154 = (f32[6,512]{1,0:T(8,128)S(1)}, f32[6,512,2048]{2,1,0:T(8,128)}) fusion(bf16[512,6,64]{0,2,1:T(8,128)(2,1)S(1)} %copy-done.32, bf16[2048,6,16]{0,2,1:T(8,128)(2,1)S(1)} %get-tuple-element.213, bf16[2048,6,48]{0,2,1:T(8,128)(2,1)S(1)} %get-tuple-element.219, pred[512,2048]{1,0:T(8,128)(4,1)S(1)} %copy-done.38), kind=kOutput, calls=%fused_computation.255 | convolution fusion | flops 827323392 | bytes 28192768 | tf_op jit(solution)/shard_map/qhd,khd->hqk/dot_general | solution.py:158
  271.5 10.5 fusion
  282.0 16.2 %multiply_reduce_fusion = (f32[6,512]{1,0:T(8,128)S(1)}, f32[6,512,2048]{2,1,0:T(8,128)}) fusion(f32[6,512,2048]{2,1,0:T(8,128)} %get-tuple-element.253, f32[6,512]{1,0:T(8,128)S(1)} %log_add_fusion, bf16[512,6,64]{0,2,1:T(8,128)(2,1)S(1)} %bitcast.135, bf16[2048,6,192]{0,2,1:T(8,128)(2,1)} %copy-done.9), kind=kOutput, calls=%fused_computation.1 | convolution fusion | flops 824177664 | bytes 52322304 | tf_op jit(solution)/shard_map/qhd,khd->hqk/dot_general | solution.py:235
  298.2 17.0 %multiply_convert_fusion = bf16[6,512,2048]{2,1,0:T(8,128)(2,1)S(1)} fusion(f32[6,512,2048]{2,1,0:T(8,128)} %get-tuple-element.255, f32[6,512,2048]{2,1,0:T(8,128)} %get-tuple-element.253, f32[6,512]{1,0:T(8,128)S(1)} %get-tuple-element.254, f32[6,512]{1,0:T(8,128)S(1)} %log_add_fusion), kind=kLoop, calls=%fused_computation | loop fusion | flops 25165824 | bytes 62939136 | tf_op jit(solution)/shard_map/convert_element_type | solution.py:239
  325.8 8.0 bitcast_add_fusion.2
  349.4 6.4 fusion.68
  355.8 11.6 %bitcast_add_fusion.1 = bf16[2048,6,64]{0,2,1:T(8,128)(2,1)S(1)} fusion(f32[2048,6,64]{0,2,1:T(8,128)} %fusion.68, bf16[512,6,64]{0,2,1:T(8,128)(2,1)S(1)} %bitcast.136, f32[6,512,2048]{2,1,0:T(8,128)} %get-tuple-element.253, f32[6,512]{1,0:T(8,128)S(1)} %log_add_fusion), kind=kOutput, calls=%fused_computation.109 | convolution fusion | flops 819462144 | bytes 30289920 | tf_op jit(solution)/shard_map/hqk,qhd->khd/dot_general | solution.py:256
  375.9 6.6 bitcast_convert_fusion
  382.5 9.3 fusion.105
  392.5 34.9 %multiply_convert_fusion.3 = (bf16[2048,1536]{1,0:T(8,128)(2,1)}, f32[2048,1536]{1,0:T(8,128)}, f32[2048,1536]{1,0:T(8,128)}) fusion(f32[1536]{0:T(1024)S(1)} %copy-done.64, bf16[2048,768]{1,0:T(8,128)(2,1)} %all-gather.11.cloned.1.call-done, bf16[768,1536]{1,0:T(8,128)(2,1)} %all-gather.13.cloned.1.call-done), kind=kOutput, calls=%fused_computation.25 | convolution fusion | flops 5039456256 | bytes 36968448 | tf_op jit(solution)/shard_map/dot_general | solution.py:195
  427.3 17.0 %convert_reduce_fusion = (f32[1536]{0:T(1024)S(1)}, bf16[2048,1536]{1,0:T(8,128)(2,1)S(1)}) fusion(f32[2048,1536]{1,0:T(8,128)} %get-tuple-element.212, bf16[2048,768]{1,0:T(8,128)(2,1)} %all-gather.17.cloned.1.call-done, bf16[768,1536]{1,0:T(8,128)(2,1)} %all-gather.15.cloned.1.call-done, f32[2048,1536]{1,0:T(8,128)} %get-tuple-element.245, ...), kind=kOutput, calls=%fused_computation.19 | convolution fusion | flops 4885314048 | bytes 36974592 | tf_op jit(solution)/shard_map/dot_general | solution.py:212
  446.9 6.4 convolution_convert_fusion
  454.0 7.7 fusion.104
  466.0 11.1 %fusion.106 = bf16[6,64,512]{2,1,0:T(8,128)(2,1)S(1)} fusion(f32[6,512,2048]{2,1,0:T(8,128)} %get-tuple-element.253, f32[6,512]{1,0:T(8,128)S(1)} %copy-done.60, f32[6,512]{1,0:T(8,128)S(1)} %copy-done.58, bf16[2048,6,192]{0,2,1:T(8,128)(2,1)} %copy-done.9), kind=kOutput, calls=%fused_computation.174 | convolution fusion | flops 824377344 | bytes 27156480 | tf_op jit(solution)/shard_map/hqk,khd->qhd/dot_general | solution.py:182
  477.2 7.3 fusion.155
  494.4 10.0 fusion.33
  504.5 9.8 fusion.156
  514.4 9.7 convolution_bitcast_fusion
  524.1 6.2 copy.69
  539.0 6.5 convert_reduce_fusion.5
  545.5 37.7 %all-reduce.25 = (f32[768]{0:T(1024)S(1)}, f32[768]{0:T(1024)S(1)}, f32[768]{0:T(1024)S(1)}, f32[768]{0:T(1024)S(1)}, f32[2304]{0:T(1024)S(1)}, /*index=5*/f32[768]{0:T(1024)S(1)}, f32[3072]{0:T(1024)S(1)}) all-reduce(f32[768]{0:T(1024)S(1)} %get-tuple-element.187, ...), channel_id=5, replica_groups=mesh['dp'=16,'tensor'=2] {'dp','tensor'}, use_global_device_ids=true, to_apply=%region_25.26.clone | all-reduce | flops 9216 | bytes 73728
  586.8 45.0 %reduce-scatter.18.cloned.1.call-done = f32[48,6,64]{2,0,1:T(8,128)} async-done(((f32[768,6,64]{2,0,1:T(8,128)}), f32[48,6,64]{2,0,1:T(8,128)}) %reduce-scatter.18.cloned.1.call-update) | async-done | bytes 73744 | tf_op jit(solution)/shard_map/reduce_scatter | solution.py:317
  631.8 141.7 %reduce-scatter.16.cloned.1.call-done = f32[48,6,192]{2,0,1:T(8,128)} async-done(((f32[768,6,192]{2,0,1:T(8,128)}), f32[48,6,192]{2,0,1:T(8,128)}) %reduce-scatter.16.cloned.1.call-update) | async-done | bytes 221200 | tf_op jit(solution)/shard_map/reduce_scatter | solution.py:316
  773.5 142.4 %reduce-scatter.20.cloned.1.call-done = f32[48,1536]{1,0:T(8,128)} async-done(((f32[768,1536]{1,0:T(8,128)}), f32[48,1536]{1,0:T(8,128)}) %reduce-scatter.20.cloned.1.call-update) | async-done | bytes 294928 | tf_op jit(solution)/shard_map/reduce_scatter | solution.py:318
  915.9 142.2 %reduce-scatter.22.cloned.1.call-done = f32[48,1536]{1,0:T(8,128)} async-done(((f32[768,1536]{1,0:T(8,128)}), f32[48,1536]{1,0:T(8,128)}) %reduce-scatter.22.cloned.1.call-update) | async-done | bytes 294928
  (314 shorter events, 143.5 us)
Async XLA Ops:
  7.2 92.2 %copy-start.3 = (bf16[1024,768]{1,0:T(8,128)(2,1)S(1)}, bf16[1024,768]{1,0:T(8,128)(2,1)}, u32[]{:S(2)}) copy-start(bf16[1024,768]{1,0:T(8,128)(2,1)} %param.35) | copy-start | bytes 4718596
  7.2 149.9 %all-gather.17.cloned.1.call-start = ((), (), s32[]{:S(2)}) async-start(), calls=%async_computation.13 | async-start | bytes 4718592 | tf_op jit(solution)/shard_map/all_gather | solution.py:211
  7.9 153.8 %all-gather.9.cloned.1.call-start = ((), (), s32[]{:S(2)}) async-start(), calls=%async_computation.8 | async-start | bytes 2506752 | tf_op jit(solution)/shard_map/all_gather | solution.py:71
  8.7 156.3 %all-gather.7.cloned.1.call-start = ((), (), s32[]{:S(2)}) async-start(), calls=%async_computation.7 | async-start | bytes 4718592 | tf_op jit(solution)/shard_map/all_gather | solution.py:125
  103.2 288.6 %all-gather.11.cloned.1.call-start = ((), (), s32[]{:S(2)}) async-start(), calls=%async_computation.9 | async-start | bytes 4718592 | tf_op jit(solution)/shard_map/all_gather | solution.py:126
  103.8 288.1 %all-gather.13.cloned.1.call-start = ((), (), s32[]{:S(2)}) async-start(), calls=%async_computation.10 | async-start | bytes 2506752 | tf_op jit(solution)/shard_map/all_gather | solution.py:73
  104.4 322.9 %all-gather.15.cloned.1.call-start = ((), (), s32[]{:S(2)}) async-start(), calls=%async_computation.11 | async-start | bytes 2506752 | tf_op jit(solution)/shard_map/all_gather | solution.py:74
  105.0 426.6 %reduce-scatter.14.cloned.1.call-start = ((), (), s32[]{:S(2)}) async-start(), calls=%async_computation.15 | async-start | bytes 4718592 | tf_op jit(solution)/shard_map/reduce_scatter | solution.py:282
  105.8 66.1 %copy-start.33 = (f32[2048,16]{0,1:T(8,128)}, f32[2048,16]{0,1:T(8,128)S(1)}, u32[]{:S(2)}) copy-start(f32[2048,16]{0,1:T(8,128)S(1)} %get-tuple-element.237) | copy-start | bytes 393220
  105.8 66.1 %copy-start.35 = (f32[2048,16]{0,1:T(8,128)}, f32[2048,16]{0,1:T(8,128)S(1)}, u32[]{:S(2)}) copy-start(f32[2048,16]{0,1:T(8,128)S(1)} %get-tuple-element.238) | copy-start | bytes 393220
  150.0 10.5 copy-start.18
  171.7 22.8 %copy-start.9 = (bf16[2048,6,192]{0,2,1:T(8,128)(2,1)}, bf16[2048,6,192]{0,2,1:T(8,128)(2,1)S(1)}, u32[]{:S(2)}) copy-start(bf16[2048,6,192]{0,2,1:T(8,128)(2,1)S(1)} %convert.33) | copy-start | bytes 14155780
  171.9 88.8 %copy-start.5 = (bf16[2048,6,48]{0,2,1:T(8,128)(2,1)}, bf16[2048,6,48]{0,2,1:T(8,128)(2,1)S(1)}, u32[]{:S(2)}) copy-start(bf16[2048,6,48]{0,2,1:T(8,128)(2,1)S(1)} %get-tuple-element.219) | copy-start | bytes 3538948
  260.7 10.8 %copy-start.8 = (f32[2048,6,64]{0,2,1:T(8,128)}, f32[2048,6,64]{0,2,1:T(8,128)S(1)}, u32[]{:S(2)}) copy-start(f32[2048,6,64]{0,2,1:T(8,128)S(1)} %fusion.61) | copy-start | bytes 9437188
  271.5 10.5 copy-start.57
  271.5 10.5 copy-start.21
  282.0 16.2 %copy-start.59 = (f32[6,512]{1,0:T(8,128)}, f32[6,512]{1,0:T(8,128)S(1)}, u32[]{:S(2)}) copy-start(f32[6,512]{1,0:T(8,128)S(1)} %fusion) | copy-start | bytes 36868
  325.8 18.1 %slice-start = ((s8[12582912]{0:T(1024)(128)(4,1)}), s8[4194304]{0:T(1024)(128)(4,1)S(1)}, s32[]{:S(2)}) async-start(s8[12582912]{0:T(1024)(128)(4,1)} %bitcast.128), calls=%async_computation.20 | async-start | bytes 8388608
  325.8 18.1 %slice-start.1 = ((s8[12582912]{0:T(1024)(128)(4,1)}), s8[4194304]{0:T(1024)(128)(4,1)S(1)}, s32[]{:S(2)}) async-start(s8[12582912]{0:T(1024)(128)(4,1)} %bitcast.128), calls=%async_computation.21 | async-start | bytes 8388608
  325.8 23.6 %slice-start.3 = ((s8[18874368]{0:T(1024)(128)(4,1)}), s8[4194304]{0:T(1024)(128)(4,1)S(1)}, s32[]{:S(2)}) async-start(s8[18874368]{0:T(1024)(128)(4,1)} %bitcast.130), calls=%async_computation.23 | async-start | bytes 8388608
  325.8 23.6 %slice-start.4 = ((s8[18874368]{0:T(1024)(128)(4,1)}), s8[4194304]{0:T(1024)(128)(4,1)S(1)}, s32[]{:S(2)}) async-start(s8[18874368]{0:T(1024)(128)(4,1)} %bitcast.130), calls=%async_computation.24 | async-start | bytes 8388608
  333.9 15.5 %slice-start.5 = ((s8[18874368]{0:T(1024)(128)(4,1)}), s8[4194304]{0:T(1024)(128)(4,1)S(1)}, s32[]{:S(2)}) async-start(s8[18874368]{0:T(1024)(128)(4,1)} %bitcast.130), calls=%async_computation.25 | async-start | bytes 8388608
  355.8 11.6 %copy-start.28 = (f32[2048,6,16]{0,2,1:T(8,128)S(1)}, f32[2048,6,16]{0,2,1:T(8,128)}, u32[]{:S(2)}) copy-start(f32[2048,6,16]{0,2,1:T(8,128)} %get-tuple-element.209) | copy-start | bytes 2359300
  391.8 139.8 %reduce-scatter.12.cloned.1.call-start = ((), (), s32[]{:S(2)}) async-start(), calls=%async_computation.14 | async-start | bytes 4718592 | tf_op jit(solution)/shard_map/reduce_scatter | solution.py:285
  427.3 19.6 %copy-start.68 = (bf16[768,1536]{1,0:T(8,128)(2,1)S(1)}, bf16[768,1536]{1,0:T(8,128)(2,1)}, u32[]{:S(2)}) copy-start(bf16[768,1536]{1,0:T(8,128)(2,1)} %all-gather.13.cloned.1.call-done) | copy-start | bytes 7077892
  453.4 85.6 %reduce-scatter.10.cloned.1.call-start = ((), (), s32[]{:S(2)}) async-start(), calls=%async_computation.12 | async-start | bytes 4718592 | tf_op jit(solution)/shard_map/reduce_scatter | solution.py:199
  466.0 11.1 %copy-start.67 = (bf16[768,1536]{1,0:T(8,128)(2,1)S(1)}, bf16[768,1536]{1,0:T(8,128)(2,1)}, u32[]{:S(2)}) copy-start(bf16[768,1536]{1,0:T(8,128)(2,1)} %all-gather.15.cloned.1.call-done) | copy-start | bytes 7077892
  489.1 142.7 %reduce-scatter.18.cloned.1.call-start = ((), (), s32[]{:S(2)}) async-start(), calls=%async_computation.17 | async-start | bytes 2506752 | tf_op jit(solution)/shard_map/reduce_scatter | solution.py:317
  494.4 279.2 %reduce-scatter.16.cloned.1.call-start = ((), (), s32[]{:S(2)}) async-start(), calls=%async_computation.16 | async-start | bytes 5013504 | tf_op jit(solution)/shard_map/reduce_scatter | solution.py:316
  504.4 411.5 %reduce-scatter.20.cloned.1.call-start = ((), (), s32[]{:S(2)}) async-start(), calls=%async_computation.18 | async-start | bytes 5013504 | tf_op jit(solution)/shard_map/reduce_scatter | solution.py:318
  514.4 543.8 %reduce-scatter.22.cloned.1.call-start = ((), (), s32[]{:S(2)}) async-start(), calls=%async_computation.19 | async-start | bytes 5013504
  583.9 474.8 %copy-start.71 = (f32[24]{0:T(128)}, f32[24]{0:T(128)S(1)}, u32[]{:S(2)}) copy-start(f32[24]{0:T(128)S(1)} %dynamic-slice.72) | copy-start | bytes 292
  (64 other events, 240.5 us)
Sparse Core Ops, SparseCore 0:
  9.6 14.8 all-gather.16
  27.1 64.0 all-gather.8
  103.4 7.9 all-gather.6
  112.8 13.2 all-gather.10
  128.8 64.0 all-gather.12
  195.5 61.1 all-gather.14
  391.9 8.2 reduce-scatter.13
  453.5 8.2 reduce-scatter.11
  489.2 7.7 reduce-scatter.9
  503.1 128.6 reduce-scatter.17
  637.6 135.9 reduce-scatter.15
  780.0 135.9 reduce-scatter.19
  921.7 136.4 reduce-scatter.21
where the time goes:
time: 1070 us
  waiting for transfers between devices  475 us (44%)
  matrix products  264 us (25%)
  blocking collectives  161 us (15%)
  other arithmetic  101 us (9%)
  local copies, waits for them, and re-layouts  46.5 us (4%)
  between operations  17.3 us (2%)
    unnamed x14, waiting for transfers between devices  145 us
    reduce_scatter x1, waiting for transfers between devices, body(): lax.psum_scatter(grad_fc, 'dp', scatter_dimension=0, tiled=True)  142 us
    reduce_scatter x1, waiting for transfers between devices, body(): lax.psum_scatter(grad_qkv, 'dp', scatter_dimension=0, tiled=True)  142 us
    unnamed x2, blocking collectives  117 us
    reduce_scatter x1, waiting for transfers between devices, body(): lax.psum_scatter(grad_dense, 'dp', scatter_dimension=0, tiled=True)  45 us
    all_gather x1, blocking collectives, body(): lax.all_gather(dense_weight, 'dp', axis=0, tiled=True)  44.1 us
    convert_element_type x4, other arithmetic, body(): grad_scores = (probs * (grad_probs - row_delta)).astype(jnp.bfloat16)  40.9 us
    dot_general x4, matrix products, body(): jnp.einsum('qhd,khd->hqk', heads_blk, value_low[:end_row], preferred_elem...  39.2 us
  transfers between devices with their start and end apart: 13, of which 4 were waited for; matrix products, arithmetic and copies ran while one was open for 37% of the time, Pallas kernels for 0%

commit v1 on v0

--- a/solution.py
+++ b/solution.py
@@ -2,6 +2,24 @@
 import jax.numpy as jnp
 from jax import lax
 from jax.sharding import PartitionSpec as P
+
+
+def gather_around(value, axis, dim):
+    ways, here, step = (lax.axis_size(axis), lax.axis_index(axis), value.shape[dim])
+    shape = [n * ways if d == dim else n for d, n in enumerate(value.shape)]
+    full = lax.dynamic_update_slice_in_dim(
+        jnp.zeros(shape, value.dtype), value, here * step, axis=dim
+    )
+    going_up = going_down = value
+    for far in range(1, ways // 2 + 1):
+        going_up = lax.ppermute(going_up, axis, [(d, (d + 1) % ways) for d in range(ways)])
+        full = lax.dynamic_update_slice_in_dim(full, going_up, (here - far) % ways * step, axis=dim)
+        if 2 * far < ways:
+            going_down = lax.ppermute(going_down, axis, [(d, (d - 1) % ways) for d in range(ways)])
+            full = lax.dynamic_update_slice_in_dim(
+                full, going_down, (here + far) % ways * step, axis=dim
+            )
+    return full
 
 
 def layout(lengths, group_rows):
@@ -69,7 +87,7 @@
     group_rows = local_rows * tensor_count
     gathered = (
         lax.all_gather(qkv_weight, "dp", axis=0, tiled=True),
-        lax.all_gather(dense_weight, "dp", axis=0, tiled=True),
+        gather_around(dense_weight, "dp", 0),
         lax.all_gather(fc_weight, "dp", axis=0, tiled=True),
         lax.all_gather(proj_weight, "dp", axis=0, tiled=True),
         lax.all_gather(attn_gain, "dp", axis=0, tiled=True),

time: 1070 us -> 1150 us (1.075)
  starting transfers between devices: 0.52 us -> 41.1 us
  local copies, waits for them, and re-layouts: 46.5 us -> 73.3 us
    ppermute x0 -> x15, starting transfers between devices: none -> 40.6 us  [the longest x7 39 us: gather_around(): lax.ppermute(going_down, axis, [(d, (d - 1) % ways) for d in range(ways)])]
    dynamic_update_slice x0 -> x16, local copies, waits for them, and re-layouts: none -> 20.5 us  [the longest x8 10.2 us: gather_around(): lax.dynamic_update_slice_in_dim(full, going_up, (here - far) % ways * ste...]
    ppermute x0 -> x15, waiting for transfers between devices: none -> 11.7 us  [the longest x8 9.52 us: gather_around(): lax.ppermute(going_up, axis, [(d, (d + 1) % ways) for d in range(ways)])]
    unnamed x188 -> x197, local copies, waits for them, and re-layouts: 34.7 us -> 35 us
  transfers between devices with their start and end apart: 13 -> 28, of which waited for: 4 -> 12; matrix products, arithmetic and copies ran while one was open for 37% -> 37% of each run, Pallas kernels for 0% -> 0%
where the time goes in v1:
time: 1150 us
  waiting for transfers between devices  485 us (42%)
  matrix products  263 us (23%)
  blocking collectives  165 us (14%)
  other arithmetic  101 us (9%)
  local copies, waits for them, and re-layouts  73.3 us (6%)
  starting transfers between devices  41.1 us (4%)
  between operations  17.9 us (2%)
    unnamed x14, waiting for transfers between devices  144 us
    reduce_scatter x1, waiting for transfers between devices, body(): lax.psum_scatter(grad_fc, 'dp', scatter_dimension=0, tiled=True)  142 us
    reduce_scatter x1, waiting for transfers between devices, body(): lax.psum_scatter(grad_qkv, 'dp', scatter_dimension=0, tiled=True)  142 us
    unnamed x2, blocking collectives  120 us
    reduce_scatter x1, waiting for transfers between devices, body(): lax.psum_scatter(grad_dense, 'dp', scatter_dimension=0, tiled=True)  45.5 us
    all_gather x1, blocking collectives, body(): lax.all_gather(dense_weight, 'dp', axis=0, tiled=True)  44.9 us
    convert_element_type x4, other arithmetic, body(): grad_scores = (probs * (grad_probs - row_delta)).astype(jnp.bfloat16)  40.4 us
    dot_general x4, matrix products, body(): jnp.einsum('qhd,khd->hqk', heads_blk, value_low[:end_row], preferred_elem...  39.2 us
  transfers between devices with their start and end apart: 28, of which 12 were waited for; matrix products, arithmetic and copies ran while one was open for 37% of the time, Pallas kernels for 0%

profile of v1, /device:TPU:0, one launch (start us, length us, event | category | flops | bytes accessed | tf_op | source)
XLA Modules:
  0.0 1146.4 jit_solution(8605995186709545158)
XLA Ops:
  18.7 79.0 %all-reduce.26 = (bf16[768]{0:T(1024)(128)(2,1)S(1)}, bf16[768]{0:T(1024)(128)(2,1)S(1)}, bf16[3072]{0:T(1024)(128)(2,1)S(1)}, bf16[768]{0:T(1024)(128)(2,1)S(1)...) all-reduce(bf16[768]{0:T(1024)(128)(2,1)S(1)} %dynamic-update-slice, ...), channel_id=1, replica_groups=mesh['dp'=16,'tensor'=2] {'dp'}, use_global_device_ids=true, to_apply=%add.14 | all-reduce | flops 9984 | bytes 39936
  114.3 44.9 %all_gather.62 = bf16[768,6,64]{2,0,1:T(8,128)(2,1)S(1)} all-gather(bf16[48,6,64]{2,0,1:T(8,128)(2,1)S(1)} %copy-done.40), channel_id=1, replica_groups=mesh['dp'=16,'tensor'=2] {'dp'}, dimensions={0}, use_global_device_ids=true | all-gather | bytes 626688 | tf_op jit(solution)/shard_map/all_gather | solution.py:225
  280.4 6.2 multiply_convert_fusion.2
  291.3 8.4 fusion.153
  299.7 9.0 fusion.2
  308.8 13.0 %multiply_reduce_fusion.1 = (f32[6,512]{1,0:T(8,128)S(1)}, f32[6,512,1536]{2,1,0:T(8,128)}) fusion(f32[6,512,1536]{2,1,0:T(8,128)} %get-tuple-element.251, f32[6,512]{1,0:T(8,128)S(1)} %log_add_fusion.1, bf16[512,6,64]{0,2,1:T(8,128)(2,1)} %bitcast.137, bf16[2048,6,192]{0,2,1:T(8,128)(2,1)} %copy-done.9), kind=kOutput, calls=%fused_computation.10 | convolution fusion | flops 618132480 | bytes 39346176 | tf_op jit(solution)/shard_map/qhd,khd->hqk/dot_general | solution.py:253
  321.8 12.9 %multiply_convert_fusion.1 = bf16[6,512,1536]{2,1,0:T(8,128)(2,1)S(1)} fusion(f32[6,512,1536]{2,1,0:T(8,128)} %get-tuple-element.257, f32[6,512,1536]{2,1,0:T(8,128)} %get-tuple-element.251, f32[6,512]{1,0:T(8,128)S(1)} %get-tuple-element.256, f32[6,512]{1,0:T(8,128)S(1)} %log_add_fusion.1), kind=kLoop, calls=%fused_computation.9 | loop fusion | flops 18874368 | bytes 47210496 | tf_op jit(solution)/shard_map/convert_element_type | solution.py:257
  340.4 10.5 fusion.154
  350.9 10.5 fusion
  361.4 16.1 %multiply_reduce_fusion = (f32[6,512]{1,0:T(8,128)S(1)}, f32[6,512,2048]{2,1,0:T(8,128)}) fusion(f32[6,512,2048]{2,1,0:T(8,128)} %get-tuple-element.253, f32[6,512]{1,0:T(8,128)S(1)} %log_add_fusion, bf16[512,6,64]{0,2,1:T(8,128)(2,1)S(1)} %bitcast.135, bf16[2048,6,192]{0,2,1:T(8,128)(2,1)} %copy-done.9), kind=kOutput, calls=%fused_computation.1 | convolution fusion | flops 824177664 | bytes 52322304 | tf_op jit(solution)/shard_map/qhd,khd->hqk/dot_general | solution.py:253
  377.5 16.7 %multiply_convert_fusion = bf16[6,512,2048]{2,1,0:T(8,128)(2,1)S(1)} fusion(f32[6,512,2048]{2,1,0:T(8,128)} %get-tuple-element.255, f32[6,512,2048]{2,1,0:T(8,128)} %get-tuple-element.253, f32[6,512]{1,0:T(8,128)S(1)} %get-tuple-element.254, f32[6,512]{1,0:T(8,128)S(1)} %log_add_fusion), kind=kLoop, calls=%fused_computation | loop fusion | flops 25165824 | bytes 62939136 | tf_op jit(solution)/shard_map/convert_element_type | solution.py:257
  404.9 8.0 bitcast_add_fusion.2
  428.4 6.4 fusion.68
  434.8 11.6 %bitcast_add_fusion.1 = bf16[2048,6,64]{0,2,1:T(8,128)(2,1)S(1)} fusion(f32[2048,6,64]{0,2,1:T(8,128)} %fusion.68, bf16[512,6,64]{0,2,1:T(8,128)(2,1)S(1)} %bitcast.136, f32[6,512,2048]{2,1,0:T(8,128)} %get-tuple-element.253, f32[6,512]{1,0:T(8,128)S(1)} %log_add_fusion), kind=kOutput, calls=%fused_computation.109 | convolution fusion | flops 819462144 | bytes 30289920 | tf_op jit(solution)/shard_map/hqk,qhd->khd/dot_general | solution.py:274
  455.1 6.6 bitcast_convert_fusion
  461.7 9.3 fusion.105
  471.6 34.8 %multiply_convert_fusion.3 = (bf16[2048,1536]{1,0:T(8,128)(2,1)}, f32[2048,1536]{1,0:T(8,128)}, f32[2048,1536]{1,0:T(8,128)}) fusion(f32[1536]{0:T(1024)S(1)} %copy-done.68, bf16[2048,768]{1,0:T(8,128)(2,1)} %all-gather.11.cloned.1.call-done, bf16[768,1536]{1,0:T(8,128)(2,1)} %all-gather.13.cloned.1.call-done), kind=kOutput, calls=%fused_computation.25 | convolution fusion | flops 5039456256 | bytes 36968448 | tf_op jit(solution)/shard_map/dot_general | solution.py:213
  506.5 17.0 %convert_reduce_fusion = (f32[1536]{0:T(1024)S(1)}, bf16[2048,1536]{1,0:T(8,128)(2,1)S(1)}) fusion(f32[2048,1536]{1,0:T(8,128)} %get-tuple-element.212, bf16[2048,768]{1,0:T(8,128)(2,1)} %all-gather.17.cloned.1.call-done, bf16[768,1536]{1,0:T(8,128)(2,1)} %all-gather.15.cloned.1.call-done, f32[2048,1536]{1,0:T(8,128)} %get-tuple-element.245, ...), kind=kOutput, calls=%fused_computation.19 | convolution fusion | flops 4885314048 | bytes 36974592 | tf_op jit(solution)/shard_map/dot_general | solution.py:230
  526.2 6.4 convolution_convert_fusion
  533.3 6.3 fusion.104
  544.4 11.2 fusion.106
  555.6 7.3 fusion.155
  572.0 10.5 fusion.33
  582.6 10.0 fusion.156
  592.7 9.8 convolution_bitcast_fusion
  602.5 6.2 copy.133
  617.4 6.5 convert_reduce_fusion.5
  623.9 40.8 %all-reduce.25 = (f32[768]{0:T(1024)S(1)}, f32[768]{0:T(1024)S(1)}, f32[768]{0:T(1024)S(1)}, f32[768]{0:T(1024)S(1)}, f32[2304]{0:T(1024)S(1)}, /*index=5*/f32[768]{0:T(1024)S(1)}, f32[3072]{0:T(1024)S(1)}) all-reduce(f32[768]{0:T(1024)S(1)} %get-tuple-element.187, ...), channel_id=5, replica_groups=mesh['dp'=16,'tensor'=2] {'dp','tensor'}, use_global_device_ids=true, to_apply=%region_25.26.clone | all-reduce | flops 9216 | bytes 73728
  668.3 45.5 %reduce-scatter.18.cloned.1.call-done = f32[48,6,64]{2,0,1:T(8,128)} async-done(((f32[768,6,64]{2,0,1:T(8,128)}), f32[48,6,64]{2,0,1:T(8,128)}) %reduce-scatter.18.cloned.1.call-update) | async-done | bytes 73744 | tf_op jit(solution)/shard_map/reduce_scatter | solution.py:335
  713.8 141.7 %reduce-scatter.16.cloned.1.call-done = f32[48,6,192]{2,0,1:T(8,128)} async-done(((f32[768,6,192]{2,0,1:T(8,128)}), f32[48,6,192]{2,0,1:T(8,128)}) %reduce-scatter.16.cloned.1.call-update) | async-done | bytes 221200 | tf_op jit(solution)/shard_map/reduce_scatter | solution.py:334
  855.5 142.2 %reduce-scatter.20.cloned.1.call-done = f32[48,1536]{1,0:T(8,128)} async-done(((f32[768,1536]{1,0:T(8,128)}), f32[48,1536]{1,0:T(8,128)}) %reduce-scatter.20.cloned.1.call-update) | async-done | bytes 294928 | tf_op jit(solution)/shard_map/reduce_scatter | solution.py:336
  997.7 141.4 %reduce-scatter.22.cloned.1.call-done = f32[48,1536]{1,0:T(8,128)} async-done(((f32[768,1536]{1,0:T(8,128)}), f32[48,1536]{1,0:T(8,128)}) %reduce-scatter.22.cloned.1.call-update) | async-done | bytes 294928
  (385 shorter events, 221.8 us)
Async XLA Ops:
  7.2 92.2 %copy-start.3 = (bf16[1024,768]{1,0:T(8,128)(2,1)S(1)}, bf16[1024,768]{1,0:T(8,128)(2,1)}, u32[]{:S(2)}) copy-start(bf16[1024,768]{1,0:T(8,128)(2,1)} %param.35) | copy-start | bytes 4718596
  7.2 229.6 %all-gather.17.cloned.1.call-start = ((), (), s32[]{:S(2)}) async-start(), calls=%async_computation.13 | async-start | bytes 4718592 | tf_op jit(solution)/shard_map/all_gather | solution.py:229
  7.9 233.7 %all-gather.9.cloned.1.call-start = ((), (), s32[]{:S(2)}) async-start(), calls=%async_computation.8 | async-start | bytes 2506752 | tf_op jit(solution)/shard_map/all_gather | solution.py:89
  8.7 236.1 %all-gather.7.cloned.1.call-start = ((), (), s32[]{:S(2)}) async-start(), calls=%async_computation.7 | async-start | bytes 4718592 | tf_op jit(solution)/shard_map/all_gather | solution.py:143
  103.2 367.8 %all-gather.11.cloned.1.call-start = ((), (), s32[]{:S(2)}) async-start(), calls=%async_computation.9 | async-start | bytes 4718592 | tf_op jit(solution)/shard_map/all_gather | solution.py:144
  103.8 367.2 %all-gather.13.cloned.1.call-start = ((), (), s32[]{:S(2)}) async-start(), calls=%async_computation.10 | async-start | bytes 2506752 | tf_op jit(solution)/shard_map/all_gather | solution.py:91
  104.4 402.1 %all-gather.15.cloned.1.call-start = ((), (), s32[]{:S(2)}) async-start(), calls=%async_computation.11 | async-start | bytes 2506752 | tf_op jit(solution)/shard_map/all_gather | solution.py:92
  104.5 54.8 %collective-permute-start = (bf16[48,6,64]{2,0,1:T(8,128)(2,1)S(1)}, bf16[48,6,64]{2,0,1:T(8,128)(2,1)S(1)}, u32[]{:S(2)}, u32[]{:S(2)}) collective-permute-start(bf16[48,6,64]{2,0,1:T(8,128)(2,1)S(1)} %copy-done.40), channel_id=1, source_target_pairs={{0,2},{2,4},{4,6},{6,8},{8,10},{10,12},{12,14},{14,16},{16,18},{18... | collective-permute-start | bytes 110600 | tf_op jit(solution)/shard_map/ppermute | solution.py:15
  104.5 56.2 %collective-permute-start.1 = (bf16[48,6,64]{2,0,1:T(8,128)(2,1)S(1)}, bf16[48,6,64]{2,0,1:T(8,128)(2,1)S(1)}, u32[]{:S(2)}, u32[]{:S(2)}) collective-permute-start(bf16[48,6,64]{2,0,1:T(8,128)(2,1)S(1)} %copy-done.40), channel_id=1, source_target_pairs={{0,30},{2,0},{4,2},{6,4},{8,6},{10,8},{12,10},{14,12},{16,14},{18,... | collective-permute-start | bytes 110600 | tf_op jit(solution)/shard_map/ppermute | solution.py:18
  110.2 499.8 %reduce-scatter.14.cloned.1.call-start = ((), (), s32[]{:S(2)}) async-start(), calls=%async_computation.15 | async-start | bytes 4718592 | tf_op jit(solution)/shard_map/reduce_scatter | solution.py:300
  159.2 8.1 collective-permute-start.2
  160.7 6.6 collective-permute-start.3
  167.3 7.9 collective-permute-start.4
  167.3 9.2 collective-permute-start.5
  175.2 9.3 collective-permute-start.6
  176.5 9.0 collective-permute-start.7
  184.6 8.4 collective-permute-start.8
  185.5 8.9 collective-permute-start.9
  192.9 8.1 collective-permute-start.10
  193.2 58.6 %copy-start.31 = (f32[2048,16]{0,1:T(8,128)}, f32[2048,16]{0,1:T(8,128)S(1)}, u32[]{:S(2)}) copy-start(f32[2048,16]{0,1:T(8,128)S(1)} %get-tuple-element.237) | copy-start | bytes 393220
  194.5 8.1 collective-permute-start.11
  201.0 8.1 collective-permute-start.12
  202.5 30.4 %collective-permute-start.13 = (bf16[48,6,64]{2,0,1:T(8,128)(2,1)}, bf16[48,6,64]{2,0,1:T(8,128)(2,1)}, u32[]{:S(2)}, u32[]{:S(2)}) collective-permute-start(bf16[48,6,64]{2,0,1:T(8,128)(2,1)} %collective-permute-done.11), channel_id=1, source_target_pairs={{0,30},{2,0},{4,2},{6,4},{8,6},{10,8},{12,10},{14,12},{16,14},{18,... | collective-permute-start | bytes 110600 | tf_op jit(solution)/shard_map/ppermute | solution.py:18
  209.0 26.3 %collective-permute-start.14 = (bf16[48,6,64]{2,0,1:T(8,128)(2,1)}, bf16[48,6,64]{2,0,1:T(8,128)(2,1)}, u32[]{:S(2)}, u32[]{:S(2)}) collective-permute-start(bf16[48,6,64]{2,0,1:T(8,128)(2,1)} %collective-permute-done.12), channel_id=1, source_target_pairs={{0,2},{2,4},{4,6},{6,8},{8,10},{10,12},{12,14},{14,16},{16,18},{18... | collective-permute-start | bytes 110600 | tf_op jit(solution)/shard_map/ppermute | solution.py:15
  251.7 88.6 %copy-start.5 = (bf16[2048,6,48]{0,2,1:T(8,128)(2,1)}, bf16[2048,6,48]{0,2,1:T(8,128)(2,1)S(1)}, u32[]{:S(2)}) copy-start(bf16[2048,6,48]{0,2,1:T(8,128)(2,1)S(1)} %get-tuple-element.219) | copy-start | bytes 3538948
  471.0 139.1 %reduce-scatter.12.cloned.1.call-start = ((), (), s32[]{:S(2)}) async-start(), calls=%async_computation.14 | async-start | bytes 4718592 | tf_op jit(solution)/shard_map/reduce_scatter | solution.py:303
  532.6 84.7 %reduce-scatter.10.cloned.1.call-start = ((), (), s32[]{:S(2)}) async-start(), calls=%async_computation.12 | async-start | bytes 4718592 | tf_op jit(solution)/shard_map/reduce_scatter | solution.py:217
  566.6 147.3 %reduce-scatter.18.cloned.1.call-start = ((), (), s32[]{:S(2)}) async-start(), calls=%async_computation.17 | async-start | bytes 2506752 | tf_op jit(solution)/shard_map/reduce_scatter | solution.py:335
  572.0 283.6 %reduce-scatter.16.cloned.1.call-start = ((), (), s32[]{:S(2)}) async-start(), calls=%async_computation.16 | async-start | bytes 5013504 | tf_op jit(solution)/shard_map/reduce_scatter | solution.py:334
  582.6 415.1 %reduce-scatter.20.cloned.1.call-start = ((), (), s32[]{:S(2)}) async-start(), calls=%async_computation.18 | async-start | bytes 5013504 | tf_op jit(solution)/shard_map/reduce_scatter | solution.py:336
  592.6 546.5 %reduce-scatter.22.cloned.1.call-start = ((), (), s32[]{:S(2)}) async-start(), calls=%async_computation.19 | async-start | bytes 5013504
  665.4 474.2 %copy-start.75 = (f32[24]{0:T(128)}, f32[24]{0:T(128)S(1)}, u32[]{:S(2)}) copy-start(f32[24]{0:T(128)S(1)} %dynamic-slice.72) | copy-start | bytes 292
  (83 other events, 573.3 us)
Sparse Core Ops, SparseCore 0:
  9.6 14.8 all-gather.16
  27.1 63.8 all-gather.8
  103.4 7.9 all-gather.6
  112.8 13.2 all-gather.10
  128.8 68.1 all-gather.12
  199.6 62.3 all-gather.14
  471.1 12.2 reduce-scatter.13
  532.7 12.2 reduce-scatter.11
  566.7 12.1 reduce-scatter.9
  585.0 128.7 reduce-scatter.17
  719.6 135.9 reduce-scatter.15
  862.0 135.6 reduce-scatter.19
  1003.4 135.5 reduce-scatter.21
